TPU v7x, 32 devices: a whole 2x2x4 slice. The times are simulated.
32 devices in a mesh: blk: 8 (over z, core), head: 4 (over y, x).
Axes of the slice: x: 2, y: 2, z: 4, core: 2. Of those that a mesh axis runs over, the one named last changes fastest.
Arguments:
- queries: bfloat16 [8192, 4096], P(('blk', 'head')), may hold values from -60 to 60
- keys: bfloat16 [8192, 4096], P(('blk', 'head')), may hold values from -6.5 to 6.5
- values: bfloat16 [8192, 4096], P(('blk', 'head')), may hold values from -6 to 6
- block_lists: int32 [32, 3], P('blk'), may hold values from 0 to 31, as said below
- block_counts: int32 [32], P('blk'), may hold values from 1 to 3, as said below
Outputs:
- attended: bfloat16 [8192, 4096], P(('blk', 'head'))
Inputs may be any that keep to these rules, and one draw needn't show every extreme that they name: `block_lists`: row q holds distinct block indices among q - 2 to q, none below 0, starting with q itself; only its first block_counts[q] entries are used, and the rest repeat q. block_counts[q] is at most min(q + 1, 3); the last block's count is 3.
All inputs are finite; a program needn't handle non-finite values.
Results may differ from a plain program's by a relative error of at most 0.0037.
Values may be sent and summed in bfloat16 or wider, within the bound.
A program may use at most 64 MiB of HBM per device.

v0:
```python
import functools
import math

import jax
import jax.numpy as jnp
from jax import lax
from jax.experimental import pallas as pl
from jax.experimental.pallas import tpu as pltpu
from jax.sharding import PartitionSpec as P

HEADS = 32
HDIM = 128
BLOCK = 256
CYCLE = 3

MESH = pl.DeviceIdType.MESH
CHUNK = 2
FARW = 1
NEARW = 1
LAG = 1
LOW = -1e30
VMEM = 67108864


def from_behind(value, axis, steps):
    count = lax.axis_size(axis)
    initial, last = (max(0, -steps), min(count, count - steps))
    return lax.ppermute(value, axis, [(source, source + steps) for source in range(initial, last)])


def by_heads(queries, keys, values, block_lists, block_counts):
    local_heads = HEADS // lax.axis_size("head")
    scale = 1.0 / HDIM**0.5
    qmine = lax.all_to_all(queries, "head", split_axis=1, concat_axis=0, tiled=True)
    kmine, vmine = (
        lax.all_to_all(keys, "head", split_axis=1, concat_axis=0, tiled=True),
        lax.all_to_all(values, "head", split_axis=1, concat_axis=0, tiled=True),
    )
    rows = qmine.shape[0]
    owned_blocks = rows // BLOCK
    reach = CYCLE - 1
    mine = jnp.stack((kmine, vmine))
    before = from_behind(mine, "blk", 1)[:, rows - reach * BLOCK :]
    extended = jnp.concatenate((before, mine), axis=1)
    own = lax.axis_index("blk")
    entry = jnp.arange(CYCLE, dtype=jnp.int32)
    frame_pos = jnp.arange(BLOCK, dtype=jnp.int32)
    causal = frame_pos[None, :] <= frame_pos[:, None]
    outputs = []
    for local in range(owned_blocks):
        target = own * owned_blocks + local
        list_row = block_lists[local]
        count = block_counts[local]
        used = entry < count
        parts_mask = []
        for place in range(CYCLE):
            distance = reach - place
            wanted = jnp.any(used & (list_row == target - distance))
            if distance == 0:
                parts_mask.append(causal & wanted)
            else:
                parts_mask.append(jnp.broadcast_to(wanted, (BLOCK, BLOCK)))
        mask = jnp.concatenate(parts_mask, axis=1)
        span = extended[:, local * BLOCK : (local + CYCLE) * BLOCK]
        qsplit = qmine[local * BLOCK : (local + 1) * BLOCK].reshape(BLOCK, local_heads, HDIM)
        ksplit = span[0].reshape(CYCLE * BLOCK, local_heads, HDIM)
        vsplit = span[1].reshape(CYCLE * BLOCK, local_heads, HDIM)
        scores = (
            jnp.einsum("qhd,khd->hqk", qsplit, ksplit, preferred_element_type=jnp.float32) * scale
        )
        scores = jnp.where(mask[None], scores, -1e30)
        top = jnp.max(scores, axis=-1, keepdims=True)
        weights = jnp.where(mask[None], jnp.exp(scores - top), 0.0)
        total = jnp.sum(weights, axis=-1)
        rounded = weights.astype(jnp.bfloat16)
        summed = jnp.einsum("hqk,khd->qhd", rounded, vsplit, preferred_element_type=jnp.float32)
        result = summed / jnp.transpose(total)[:, :, None]
        outputs.append(result.reshape(BLOCK, local_heads * HDIM).astype(jnp.bfloat16))
    joined = jnp.concatenate(outputs, axis=0)
    return lax.all_to_all(joined, "head", split_axis=0, concat_axis=1, tiled=True)


def kernel(
    width, runs, chunk, far_window, near_window, lag,
    lists_far, counts_far, queries, keys, values, out,
    lists, counts, q_mine, k_mine, v_mine, one_k, one_v, two_k, two_v, o_mine,
    local_sem, out_sem, far_send, far_recv, near_send, near_recv,
):
    across = chunk * HDIM
    chunks = HEADS // chunk
    blk, head = lax.axis_index("blk"), lax.axis_index("head")
    me = blk * width + head
    total = runs * width
    even = lax.rem(head, 2) == 0

    def at(step):
        moved = me + step
        return (lax.div(moved, width), lax.rem(moved, width))

    ahead, behind = me + 2 < total, me >= 2
    partner = (blk, jnp.where(even, head + 1, head - 1))

    barrier = pltpu.get_barrier_semaphore()
    pl.semaphore_signal(barrier, inc=1, device_id=partner, device_id_type=MESH)

    @pl.when(ahead)
    def _():
        pl.semaphore_signal(barrier, inc=1, device_id=at(2), device_id_type=MESH)

    @pl.when(behind)
    def _():
        pl.semaphore_signal(barrier, inc=1, device_id=at(-2), device_id_type=MESH)

    loads = [
        pltpu.make_async_copy(source, target, local_sem.at[i])
        for i, (source, target) in enumerate((
            (lists_far, lists), (counts_far, counts), (queries, q_mine), (keys, k_mine), (values, v_mine)
        ))
    ]
    for load in loads:
        load.start()

    pl.semaphore_wait(barrier, 1 + ahead.astype(jnp.int32) + behind.astype(jnp.int32))

    def columns(c):
        return pl.ds(pl.multiple_of(c * across, across), across)

    def far(c):
        return [
            pltpu.make_async_remote_copy(
                src_ref=source.at[:, columns(c)], dst_ref=target.at[c],
                send_sem=far_send.at[i, c], recv_sem=far_recv.at[i, c],
                device_id=at(2), device_id_type=MESH,
            )
            for i, (source, target) in enumerate(((keys, two_k), (values, two_v)))
        ]

    def near_own(c):
        return [
            pltpu.make_async_remote_copy(
                src_ref=source.at[:, columns(c)], dst_ref=target.at[c],
                send_sem=near_send.at[i, c], recv_sem=near_recv.at[i, c],
                device_id=partner, device_id_type=MESH,
            )
            for i, (source, target) in enumerate(((keys, one_k), (values, one_v)))
        ]

    def near_pass(c):
        return [
            pltpu.make_async_remote_copy(
                src_ref=source.at[c], dst_ref=target.at[c],
                send_sem=near_send.at[i, c], recv_sem=near_recv.at[i, c],
                device_id=partner, device_id_type=MESH,
            )
            for i, (source, target) in enumerate(((two_k, one_k), (two_v, one_v)))
        ]

    def send_far(c):
        @pl.when(ahead)
        def _():
            for copy in far(c):
                copy.start()

    def send_near(c):
        @pl.when(even)
        def _():
            for copy in near_own(c):
                copy.start()

    for c in range(max(far_window, near_window)):
        if c < far_window:
            send_far(c)
        if c < near_window:
            send_near(c)

    @pl.when(jnp.logical_not(behind))
    def _():
        two_k[...] = jnp.zeros_like(two_k)
        two_v[...] = jnp.zeros_like(two_v)

    @pl.when(me == 0)
    def _():
        one_k[...] = jnp.zeros_like(one_k)
        one_v[...] = jnp.zeros_like(one_v)

    for load in loads:
        load.wait()

    def wanted(distance):
        found = False
        for place in range(CYCLE):
            hit = jnp.logical_and(place < counts[head], lists[head, place] == me - distance)
            found = jnp.logical_or(found, hit)
        return found

    shape = (BLOCK, BLOCK)
    causal = lax.broadcasted_iota(jnp.int32, shape, 1) <= lax.broadcasted_iota(jnp.int32, shape, 0)
    bias_own = jnp.where(jnp.logical_and(causal, wanted(0)), 0.0, LOW)
    bias_one = jnp.where(wanted(1), 0.0, LOW)
    bias_two = jnp.where(wanted(2), 0.0, LOW)
    rate = math.log2(math.e) / math.sqrt(HDIM)

    def attend(c):
        for h in range(chunk):
            mine = pl.ds(pl.multiple_of(c * across + h * HDIM, HDIM), HDIM)
            held = slice(h * HDIM, (h + 1) * HDIM)
            q = q_mine[:, mine]

            def score(k):
                return lax.dot_general(q, k, (((1,), (1,)), ((), ())), preferred_element_type=jnp.float32)

            own = score(k_mine[:, mine]) + bias_own
            one = score(one_k[c, :, held])
            two = score(two_k[c, :, held])
            top = jnp.maximum(
                jnp.max(own, axis=1, keepdims=True),
                jnp.maximum(
                    jnp.max(one, axis=1, keepdims=True) + bias_one,
                    jnp.max(two, axis=1, keepdims=True) + bias_two,
                ),
            )
            own = jnp.exp2((own - top) * rate)
            one = jnp.exp2((one - (top - bias_one)) * rate)
            two = jnp.exp2((two - (top - bias_two)) * rate)
            weight = jnp.sum(own + one + two, axis=1, keepdims=True)

            def part(w, v):
                return jnp.dot(w.astype(jnp.bfloat16), v, preferred_element_type=jnp.float32)

            summed = part(own, v_mine[:, mine]) + part(one, one_v[c, :, held]) + part(two, two_v[c, :, held])
            o_mine[:, mine] = (summed / weight).astype(o_mine.dtype)

    def result(c):
        return pltpu.make_async_copy(o_mine.at[:, columns(c)], out.at[:, columns(c)], out_sem.at[c])

    def move(c):
        far_copies, own, passed = far(c), near_own(c), near_pass(c)
        far_next, own_next = far(c + far_window), near_own(c + near_window)
        for i in range(2):
            @pl.when(behind)
            def _():
                far_copies[i].wait_recv()

            @pl.when(jnp.logical_and(jnp.logical_not(even), behind))
            def _():
                passed[i].start()

            @pl.when(ahead)
            def _():
                far_copies[i].wait_send()

            @pl.when(jnp.logical_and(ahead, c + far_window < chunks))
            def _():
                far_next[i].start()

            @pl.when(even)
            def _():
                own[i].wait_send()

            @pl.when(jnp.logical_and(even, c + near_window < chunks))
            def _():
                own_next[i].start()

    def work(c):
        @pl.when(me >= 1)
        def _():
            for copy in near_pass(c):
                copy.wait_recv()

        attend(c)
        result(c).start()

    def step(t, carry):
        @pl.when(t < chunks)
        def _():
            move(t)

        @pl.when(t >= lag)
        def _():
            work(t - lag)

        return carry

    lax.fori_loop(0, chunks + lag, step, 0)

    def finish(c, carry):
        result(c).wait()

        @pl.when(jnp.logical_and(jnp.logical_not(even), behind))
        def _():
            for copy in near_pass(c):
                copy.wait_send()

        return carry

    lax.fori_loop(0, chunks, finish, 0)


def by_blocks(width, runs, queries, keys, values, block_lists, block_counts):
    chunks = HEADS // CHUNK
    across = CHUNK * HDIM
    whole = pltpu.VMEM(queries.shape, jnp.bfloat16)
    landing = pltpu.VMEM((chunks, BLOCK, across), jnp.bfloat16)
    return pl.pallas_call(
        functools.partial(kernel, width, runs, CHUNK, FARW, NEARW, LAG),
        out_shape=jax.ShapeDtypeStruct(queries.shape, jnp.bfloat16),
        in_specs=[pl.BlockSpec(memory_space=pltpu.HBM)] * 5,
        out_specs=pl.BlockSpec(memory_space=pltpu.HBM),
        scratch_shapes=[
            pltpu.SMEM(block_lists.shape, jnp.int32), pltpu.SMEM(block_counts.shape, jnp.int32),
            whole, whole, whole, landing, landing, landing, landing, whole,
            pltpu.SemaphoreType.DMA((5,)),
            pltpu.SemaphoreType.DMA((chunks,)),
            pltpu.SemaphoreType.DMA((2, chunks)),
            pltpu.SemaphoreType.DMA((2, chunks)),
            pltpu.SemaphoreType.DMA((2, chunks)),
            pltpu.SemaphoreType.DMA((2, chunks)),
        ],
        compiler_params=pltpu.CompilerParams(
            collective_id=0, has_side_effects=True, vmem_limit_bytes=VMEM
        ),
    )(block_lists, block_counts, queries, keys, values)


def solution(mesh):
    width, runs = mesh.shape["head"], mesh.shape["blk"]

    def body(queries, keys, values, block_lists, block_counts):
        if queries.shape[0] == BLOCK and width % 2 == 0:
            return by_blocks(width, runs, queries, keys, values, block_lists, block_counts)
        return by_heads(queries, keys, values, block_lists, block_counts)

    return jax.shard_map(
        body,
        mesh=mesh,
        in_specs=(
            P(("blk", "head"), None),
            P(("blk", "head"), None),
            P(("blk", "head"), None),
            P("blk", None),
            P("blk"),
        ),
        out_specs=P(("blk", "head"), None),
        check_vma=False,
    )
```

profile of v0, /device:TPU:17, one launch (start us, length us, event | category | flops | bytes accessed | tf_op | source)
XLA Modules:
  0.0 104.9 jit_solution(17450902052564013768)
XLA Ops:
  0.0 101.7 %shard_map.55 = bf16[256,4096]{1,0:T(8,128)(2,1)} custom-call(s32[4,3]{1,0:T(4,128)} %lists_far.1, s32[4]{0:T(128)} %counts_far.1, bf16[256,4096]{1,0:T(8,128)(2,1)} %queries.1, bf16[256,4096]{1,0:T(8,128)(2,1)} %keys.1, bf16[256,4096]{1,0:T(8,128)(2,1)} %values.1), custom_call_target="tpu_custom_call" | custom-call | tf_op jit(solution)/shard_map/pallas_call | solution.py:304
  101.7 3.1 %copy.7 = bf16[256,4096]{1,0:T(8,128)(2,1)} copy(bf16[256,4096]{1,0:T(8,128)(2,1)} %shard_map.55) | data formatting | bytes 4194304
where the time goes:
time: 105 us
  Pallas kernels  102 us (97%)
  local copies, waits for them, and re-layouts  3.13 us (3%)
    pallas_call x1, Pallas kernels, by_blocks(): pl.pallas_call(functools.partial(kernel, width, runs, CHUNK, FARW, NEARW,...  102 us
    unnamed x1, local copies, waits for them, and re-layouts  3.13 us

commit v1 on v0

--- a/solution.py
+++ b/solution.py
@@ -237,12 +237,9 @@
         far_copies, own, passed = far(c), near_own(c), near_pass(c)
         far_next, own_next = far(c + far_window), near_own(c + near_window)
         for i in range(2):
-            @pl.when(behind)
+            @pl.when(jnp.logical_and(jnp.logical_not(even), behind))
             def _():
                 far_copies[i].wait_recv()
-
-            @pl.when(jnp.logical_and(jnp.logical_not(even), behind))
-            def _():
                 passed[i].start()
 
             @pl.when(ahead)
@@ -262,6 +259,11 @@
                 own_next[i].start()
 
     def work(c):
+        @pl.when(jnp.logical_and(even, behind))
+        def _():
+            for copy in far(c):
+                copy.wait_recv()
+
         @pl.when(me >= 1)
         def _():
             for copy in near_pass(c):

time: 105 us -> 105 us (level)
  no operation moved by 1% of the time
where the time goes in v1:
time: 105 us
  Pallas kernels  102 us (97%)
  local copies, waits for them, and re-layouts  3.13 us (3%)
    pallas_call x1, Pallas kernels, by_blocks(): pl.pallas_call(functools.partial(kernel, width, runs, CHUNK, FARW, NEARW,...  102 us
    unnamed x1, local copies, waits for them, and re-layouts  3.13 us

profile of v1, /device:TPU:17, one launch (start us, length us, event | category | flops | bytes accessed | tf_op | source)
XLA Modules:
  0.0 104.9 jit_solution(7283147515804085742)
XLA Ops:
  0.0 101.7 %shard_map.55 = bf16[256,4096]{1,0:T(8,128)(2,1)} custom-call(s32[4,3]{1,0:T(4,128)} %lists_far.1, s32[4]{0:T(128)} %counts_far.1, bf16[256,4096]{1,0:T(8,128)(2,1)} %queries.1, bf16[256,4096]{1,0:T(8,128)(2,1)} %keys.1, bf16[256,4096]{1,0:T(8,128)(2,1)} %values.1), custom_call_target="tpu_custom_call" | custom-call | tf_op jit(solution)/shard_map/pallas_call | solution.py:306
  101.7 3.1 %copy.7 = bf16[256,4096]{1,0:T(8,128)(2,1)} copy(bf16[256,4096]{1,0:T(8,128)(2,1)} %shard_map.55) | data formatting | bytes 4194304
